TPU v7x, 256 devices: a whole 4x4x8 slice. The times are simulated.
256 devices in a mesh: dp: 4 (over z_lo, core), fsdp: 64 (over x, z_hi, y).
Axes of the slice: x: 4, y: 4, z: 8 (z_hi: 4, z_lo: 2; z = z_hi * 2 + z_lo), core: 2. Of those that a mesh axis runs over, the one named last changes fastest.
Arguments:
- inputs: bfloat16 [256, 768, 4608], P(('dp', 'fsdp')), may hold values from -24 to 24
- cotangent: bfloat16 [256, 768, 1024], P(('dp', 'fsdp')), may hold values from -6 to 6
- response_mask: int32 [256, 768], P(('dp', 'fsdp')), may hold values from 0 to 1, as said below
- policy: float32 [4608, 1024], P('fsdp'), may hold values from -0.09375 to 0.09375
- anchor: float32 [4608, 1024], P('fsdp'), may hold values from -0.09375 to 0.09375
Outputs:
- gradient: float32 [4608, 1024], P('fsdp')
- anchor_next: float32 [4608, 1024], P('fsdp')
Inputs may be any that keep to these rules, and one draw needn't show every extreme that they name: `response_mask`: each sequence is a prompt of 96 to 383 tokens, then a run of response tokens of length at least 768/4 (cut at the sequence's end), then padding.
All inputs are finite; a program needn't handle non-finite values.
Results may differ from a plain program's by a relative error of at most 0.0029.
Values may be sent and summed in bfloat16 or wider, within the bound.
A program may use at most 128 MiB of HBM per device.

v0:
```python
import jax
import jax.numpy as jnp
from jax import lax
from jax.sharding import PartitionSpec as P

kl_weight = 0.5
ema_rate = 0.01
step_size = 0.1


def shards(inputs, cotangent, response_mask, policy, anchor):
    seq_dev, seq_len, width = inputs.shape
    kv_width = cotangent.shape[2]
    tokens_flat = inputs.reshape(seq_dev * seq_len, width)
    delta = (policy - anchor).astype(jnp.bfloat16)
    columns = tokens_flat
    spread = jnp.dot(
        columns,
        lax.all_gather(delta, "fsdp", axis=0, tiled=True),
        preferred_element_type=jnp.float32,
    )
    spread = spread.reshape(seq_dev, seq_len, kv_width)
    weights_mask = response_mask.astype(jnp.float32)
    counted = jnp.sum(weights_mask, axis=1)
    signal = (
        weights_mask[:, :, None]
        * (cotangent.astype(jnp.float32) + kl_weight * spread)
        / counted[:, None, None]
    )
    signal = signal.astype(jnp.bfloat16).reshape(seq_dev * seq_len, kv_width)
    columns = tokens_flat
    local_rows = lax.psum_scatter(
        lax.dot_general(
            columns, signal, (((0,), (0,)), ((), ())), preferred_element_type=jnp.float32
        ),
        "fsdp",
        scatter_dimension=0,
        tiled=True,
    )
    gradient = lax.psum(local_rows, "dp")
    anchor_next = (1.0 - ema_rate) * anchor + ema_rate * (policy - step_size * gradient)
    return (gradient, anchor_next)


def solution(mesh):
    placed = (
        P(("dp", "fsdp"), None, None),
        P(("dp", "fsdp"), None, None),
        P(("dp", "fsdp"), None),
        P("fsdp", None),
        P("fsdp", None),
    )
    return jax.shard_map(
        shards,
        mesh=mesh,
        in_specs=placed,
        out_specs=(P("fsdp", None), P("fsdp", None)),
        check_vma=False,
    )
```

profile of v0, /device:TPU:1, one launch (start us, length us, event | category | flops | bytes accessed | tf_op | source)
XLA Modules:
  0.0 515.4 jit_solution(17863956818700483077)
XLA Ops:
  7.2 0.0 copy-start.3
  7.2 0.0 all-gather.2.cloned.1.call-start
  7.2 1.7 subtract_convert_fusion
  9.0 0.0 all-gather.2.cloned.1.call-update
  9.0 0.0 reduce-scatter.4.cloned.1.call-start
  9.0 1.7 copy.12
  10.8 0.0 copy-done.3
  10.8 0.6 convert_reduce_fusion.1
  11.4 118.7 %all-gather.2.cloned.1.call-done = bf16[4608,1024]{1,0:T(8,128)(2,1)} async-done(((bf16[72,1024]{1,0:T(8,128)(2,1)}), bf16[4608,1024]{1,0:T(8,128)(2,1)}) %all-gather.2.cloned.1.call-update) | async-done | bytes 9437200 | tf_op jit(solution)/shard_map/all_gather | solution.py:19
  130.1 14.3 %fusion.5 = bf16[1,768,1024]{1,2,0:T(8,128)(2,1)S(1)} fusion(bf16[1,768,1024]{1,2,0:T(8,128)(2,1)S(1)} %copy.12, bf16[4608,1024]{1,0:T(8,128)(2,1)} %all-gather.2.cloned.1.call-done, bf16[1,768,4608]{2,1,0:T(8,128)(2,1)} %param.5, f32[]{:T(128)} %get-tuple-element.7, f32[768]{0:T(1024)S(1)} %get-tuple-element.6), kind=kOutput, calls=%fused_computation.7 | convolution fusion | flops 7252475904 | bytes 19663876 | tf_op jit(solution)/shard_map/dot_general | solution.py:17
  144.4 10.6 %convolution_bitcast_fusion = f32[4608,1024]{0,1:T(8,128)} fusion(bf16[1,768,4608]{2,1,0:T(8,128)(2,1)S(1)} %copy-done.4, bf16[1,768,1024]{1,2,0:T(8,128)(2,1)S(1)} %fusion.5), kind=kOutput, calls=%fused_computation | convolution fusion | flops 7247757312 | bytes 27525120 | tf_op jit(solution)/shard_map/dot_general | solution.py:33
  155.0 18.6 %copy.17 = f32[4608,1024]{1,0:T(8,128)} copy(f32[4608,1024]{0,1:T(8,128)} %convolution_bitcast_fusion) | data formatting | bytes 37748736
  173.7 0.0 reduce-scatter.4.cloned.1.call-update
  173.7 0.0 all-reduce.2.cloned.1.call-start
  173.8 288.4 %reduce-scatter.4.cloned.1.call-done = f32[72,1024]{1,0:T(8,128)} async-done(((f32[4608,1024]{1,0:T(8,128)}), f32[72,1024]{1,0:T(8,128)}) %reduce-scatter.4.cloned.1.call-update) | async-done | bytes 294928
  462.1 2.0 copy.18
  464.1 0.0 all-reduce.2.cloned.1.call-update
  464.1 0.0 copy-done.1
  464.1 0.2 copy.13
  464.3 0.2 copy.14
  464.5 41.3 %all-reduce.2.cloned.1.call-done = f32[72,1024]{0,1:T(8,128)} async-done(((f32[72,1024]{0,1:T(8,128)}), f32[72,1024]{0,1:T(8,128)}) %all-reduce.2.cloned.1.call-update) | async-done | bytes 294928 | tf_op jit(solution)/shard_map/psum | solution.py:40
  505.8 1.2 multiply_add_fusion
  507.1 0.9 copy.16
  508.0 0.9 copy.15
  (7 shorter events, 0.0 us)
Async XLA Ops:
  7.2 3.6 copy-start.3
  7.2 122.9 %all-gather.2.cloned.1.call-start = ((), (), s32[]{:S(2)}) async-start(), calls=%async_computation.1 | async-start | bytes 9584640 | tf_op jit(solution)/shard_map/all_gather | solution.py:19
  9.0 453.1 %reduce-scatter.4.cloned.1.call-start = ((), (), s32[]{:S(2)}) async-start(), calls=%async_computation.3 | async-start | bytes 19169280
  130.1 14.3 %copy-start.4 = (bf16[1,768,4608]{2,1,0:T(8,128)(2,1)S(1)}, bf16[1,768,4608]{2,1,0:T(8,128)(2,1)}, u32[]{:S(2)}) copy-start(bf16[1,768,4608]{2,1,0:T(8,128)(2,1)} %param.5) | copy-start | bytes 21233668
  173.7 290.4 %copy-start.1 = (f32[72,1024]{1,0:T(8,128)S(1)}, f32[72,1024]{1,0:T(8,128)}, u32[]{:S(2)}) copy-start(f32[72,1024]{1,0:T(8,128)} %param.9) | copy-start | bytes 884740
  173.7 290.6 %copy-start.2 = (f32[72,1024]{1,0:T(8,128)S(1)}, f32[72,1024]{1,0:T(8,128)}, u32[]{:S(2)}) copy-start(f32[72,1024]{1,0:T(8,128)} %param.8) | copy-start | bytes 884740
  173.7 332.1 %all-reduce.2.cloned.1.call-start = ((), (), s32[]{:S(2)}) async-start(), calls=%async_computation.2 | async-start | bytes 1048576 | tf_op jit(solution)/shard_map/psum | solution.py:40
  505.8 2.1 copy-start
Sparse Core Ops, SparseCore 0:
  11.8 118.2 all-gather.1
  173.8 288.2 reduce-scatter.3
  465.0 40.8 all-reduce.1
where the time goes:
time: 516 us; the launch traced here: 515 us
  waiting for transfers between devices  448 us (87%)
  matrix products  24.9 us (5%)
  local copies, waits for them, and re-layouts  24.5 us (5%)
  between operations  13.8 us (3%)
    unnamed x4, waiting for transfers between devices  288 us
    all_gather x1, waiting for transfers between devices, shards(): lax.all_gather(delta, 'fsdp', axis=0, tiled=True)  119 us
    psum x1, waiting for transfers between devices, shards(): gradient = lax.psum(local_rows, 'dp')  41.3 us
    unnamed x17, local copies, waits for them, and re-layouts  24.5 us
    dot_general x1, matrix products, shards(): jnp.dot(columns, lax.all_gather(delta, 'fsdp', axis=0, tiled=True), prefe...  14.3 us
    dot_general x1, matrix products, shards(): lax.dot_general(columns, signal, (((0,), (0,)), ((), ())), preferred_elem...  10.6 us
  transfers between devices with their start and end apart: 3, of which 3 were waited for; matrix products, arithmetic and copies ran while one was open for 1% of the time, Pallas kernels for 0%

commit v1 on v0

v1 whole, which is shorter than its diff:
```python
import functools

import jax
import jax.numpy as jnp
from jax import lax
from jax.experimental import pallas as pl
from jax.experimental.pallas import tpu as pltpu
from jax.sharding import PartitionSpec as P

kl_weight = 0.5
ema_rate = 0.01
step_size = 0.1

MESH = pl.DeviceIdType.MESH
F32 = jnp.float32
BF16 = jnp.bfloat16

LEN = 768
D = 4608
KVW = 1024
HALF = KVW // 2
ROWS = 72
SLAB = 16 * ROWS
PACK = 2 * ROWS
ORDER = (2, 1, 3, 0)


def kernel(x_hbm, cot_hbm, mask_ref, policy_ref, anchor_ref, grad_ref, next_ref,
           xv, ta, tb, stage, dcol, spread, cot, sig_t, scale, gn, ga, gb, ra, rb,
           ha, hb, ha16, hb16, r2a, r2b, js, js16, zr, zsum, fin,
           loc, sib_s, sib_r, p1_s, p1_r, p2_s, p2_r, p3a_s, p3a_r, p3b_s, p3b_r,
           q1a_s, q1a_r, q1b_s, q1b_r, q2_s, q2_r, q3_s, q3_r, q4_s, q4_r):
    dp, fs = lax.axis_index("dp"), lax.axis_index("fsdp")
    c, zl = dp % 2, dp // 2
    x, zh, y = fs // 16, (fs // 4) % 4, fs % 4
    z = zh * 2 + zl

    def at(c_, x_, y_, z_):
        return ((z_ % 2) * 2 + c_, (x_ * 4 + z_ // 2) * 4 + y_)

    def on_x(k):
        return at(c, (x + k) % 4, y, z)

    def on_y(k):
        return at(c, x, (y + k) % 4, z)

    def on_z(k):
        return at(c, x, y, (z + k) % 8)

    sibling = at(1 - c, x, y, z)
    partner = at(c, x, y, zh * 2 + (1 - zl))
    diagonal = at(1 - c, x, y, zh * 2 + (1 - zl))

    sends = []

    def push(src, dst, ssem, rsem, device):
        copy = pltpu.make_async_remote_copy(
            src_ref=src, dst_ref=dst, send_sem=ssem, recv_sem=rsem,
            device_id=device, device_id_type=MESH)
        copy.start()
        sends.append(copy)
        return copy

    own_x = pltpu.make_async_copy(x_hbm.at[0], xv.at[pl.ds(0, LEN)], loc.at[0])
    own_x.start()
    mine = pl.multiple_of(c * HALF, HALF)
    other = pl.multiple_of((1 - c) * HALF, HALF)
    own_cot = pltpu.make_async_copy(
        cot_hbm.at[0, :, pl.ds(mine, HALF)], cot.at[pl.ds(0, LEN)], loc.at[1])
    own_cot.start()

    barrier = pltpu.get_barrier_semaphore()
    peers = [on_x(k) for k in (1, 2, 3)] + [on_y(k) for k in (1, 2, 3)]
    peers += [on_z(k) for k in range(1, 8)] + [sibling, diagonal]
    for device in peers:
        pl.semaphore_signal(barrier, inc=1, device_id=device, device_id_type=MESH)

    delta = policy_ref[...] - anchor_ref[...]
    delta = jnp.where(c == 0, delta[:, :HALF], delta[:, HALF:])
    blocks = [delta[:, 128 * i:128 * (i + 1)] for i in range(4)]
    ta[x, y, zh] = jnp.concatenate(blocks[:2], axis=0).astype(BF16)
    tb[y, x, zh] = jnp.concatenate(blocks[2:], axis=0).astype(BF16)
    weights = mask_ref[...].astype(F32)
    weights = weights / jnp.sum(weights, axis=1, keepdims=True)
    scale[0] = jnp.broadcast_to(weights, (8, LEN))

    pl.semaphore_wait(barrier, len(peers))

    p1 = []
    for k in (1, 2, 3):
        device = on_z(jnp.where(zl == 1, k, 8 - k))
        p1.append(push(ta.at[x, y, zh], ta.at[x, y, zh], p1_s.at[0, k - 1], p1_r.at[0, k - 1], device))
        p1.append(push(tb.at[y, x, zh], tb.at[y, x, zh], p1_s.at[1, k - 1], p1_r.at[1, k - 1], device))

    sib = [
        push(x_hbm.at[0], xv.at[pl.ds(LEN, LEN)], sib_s.at[0], sib_r.at[0], sibling),
        push(cot_hbm.at[0, :, pl.ds(other, HALF)], cot.at[pl.ds(LEN, LEN)], sib_s.at[1], sib_r.at[1], sibling),
        push(scale.at[0], scale.at[1], sib_s.at[2], sib_r.at[2], sibling),
    ]

    for copy in p1:
        copy.wait_recv()
    p2 = []
    for k in (1, 2, 3):
        p2.append(push(ta.at[x, y], ta.at[x, y], p2_s.at[0, k - 1], p2_r.at[0, k - 1], on_y(k)))
        p2.append(push(tb.at[y, x], tb.at[y, x], p2_s.at[1, k - 1], p2_r.at[1, k - 1], on_x(k)))

    spread[...] = jnp.zeros_like(spread)
    for copy in p2:
        copy.wait_recv()
    p3a, p3b = [], []
    for k in (1, 2, 3):
        p3a.append(push(ta.at[x], ta.at[x], p3a_s.at[k - 1], p3a_r.at[k - 1], on_x(k)))
    for j in range(4):
        xs = (x + j) % 4
        p3b.append([push(tb.at[y, xs], tb.at[y, xs], p3b_s.at[j, k - 1], p3b_r.at[j, k - 1], on_y(k))
                    for k in (1, 2, 3)])

    own_x.wait()
    own_cot.wait()
    for copy in sib:
        copy.wait_recv()

    def first_product(load, xs, part):
        def unpack(i, carry):
            v = load(i // 4, i % 4).astype(F32)
            row = pl.ds(pl.multiple_of((i % 4) * 288 + (i // 4) * ROWS, 8), ROWS)
            stage[row, 0:128] = v[:ROWS]
            stage[row, 128:256] = v[ROWS:]
            return carry
        lax.fori_loop(0, 16, unpack, 0)
        dcol[...] = stage[...].astype(BF16)

        def tokens(m, carry):
            rows = pl.ds(pl.multiple_of(m * 512, 512), 512)
            lhs = xv[rows, pl.ds(pl.multiple_of(xs * SLAB, 128), SLAB)]
            spread[rows, part * 256:(part + 1) * 256] += jnp.dot(lhs, dcol[...], preferred_element_type=F32)
            return carry
        lax.fori_loop(0, 3, tokens, 0)

    def product_a(xs):
        first_product(lambda yy, zz: ta[xs, yy, zz], xs, 0)

    def product_b(xs):
        first_product(lambda yy, zz: tb[yy, xs, zz], xs, 1)

    def ready_b(j):
        for copy in p3b[j]:
            copy.wait_recv()
        product_b((x + j) % 4)

    def ready_a(k):
        p3a[k - 1].wait_recv()
        product_a((x + 4 - k) % 4)

    product_a(x)
    ready_b(0)
    ready_b(1)
    ready_a(1)
    ready_a(3)
    ready_b(2)
    ready_a(2)
    ready_b(3)

    def make_signal(m, carry):
        rows = pl.ds(pl.multiple_of(m * 256, 256), 256)
        u = cot[rows, :].astype(F32) + kl_weight * spread[rows, :]
        lane = pl.ds(pl.multiple_of((m % 3) * 256, 256), 256)
        w = scale[m // 3, 0:1, lane]
        sig_t[:, rows] = (u.T * w).astype(BF16)
        return carry
    lax.fori_loop(0, 6, make_signal, 0)

    def natural(xs, yy, zz):
        return pl.ds(pl.multiple_of(xs * SLAB + zz * 288 + yy * ROWS, 8), ROWS)

    def own(rows, part):
        return jnp.concatenate([gn[rows, part * 256:part * 256 + 128],
                                gn[rows, part * 256 + 128:part * 256 + 256]], axis=0)

    q1a = [None] * 3
    q1b = [None] * 4
    for i, off in enumerate(ORDER):
        xs = (x + off) % 4
        out = jnp.dot(sig_t[...], xv[:, pl.ds(pl.multiple_of(xs * SLAB, 128), SLAB)],
                      preferred_element_type=F32)
        gn[pl.ds(pl.multiple_of(xs * SLAB, 8), SLAB), :] = out.T

        def pack_b(n, carry):
            yy, zz = (y + 1 + n // 4) % 4, n % 4
            gb[yy, xs, zz] = own(natural(xs, yy, zz), 1).astype(BF16)
            return carry
        lax.fori_loop(0, 12, pack_b, 0)
        q1b[i] = [push(gb.at[(y + k) % 4, xs], rb.at[k - 1, xs], q1b_s.at[i, k - 1], q1b_r.at[i, k - 1], on_y(k))
                  for k in (2, 1, 3)]
        if off:
            def pack_a(n, carry):
                yy, zz = n // 4, n % 4
                ga[xs, yy, zz] = own(natural(xs, yy, zz), 0).astype(BF16)
                return carry
            lax.fori_loop(0, 16, pack_a, 0)
            q1a[off - 1] = push(ga.at[xs], ra.at[off - 1], q1a_s.at[off - 1], q1a_r.at[off - 1], on_x(off))

    q2 = []
    for i, off in enumerate(ORDER):
        xs = (x + off) % 4
        for copy in q1b[i]:
            copy.wait_recv()

        def sum_b(zz, carry):
            t = own(natural(xs, y, zz), 1)
            for k in range(3):
                t = t + rb[k, xs, zz].astype(F32)
            hb[xs, zz] = t
            hb16[xs, zz] = t.astype(BF16)
            return carry
        lax.fori_loop(0, 4, sum_b, 0)
        if off:
            q2.append(push(hb16.at[xs], r2b.at[off - 1], q2_s.at[1, off - 1], q2_r.at[1, off - 1], on_x(off)))

    for copy in q1a:
        copy.wait_recv()
    for off in ORDER:
        yy = (y + off) % 4

        def sum_a(zz, carry):
            t = own(natural(x, yy, zz), 0)
            for k in range(3):
                t = t + ra[k, yy, zz].astype(F32)
            ha[yy, zz] = t
            ha16[yy, zz] = t.astype(BF16)
            return carry
        lax.fori_loop(0, 4, sum_a, 0)
        if off:
            q2.append(push(ha16.at[yy], r2a.at[off - 1], q2_s.at[0, off - 1], q2_r.at[0, off - 1], on_y(off)))

    for copy in q2:
        copy.wait_recv()

    def sum_2(zz, carry):
        a, b = ha[y, zz], hb[x, zz]
        for k in range(3):
            a = a + r2a[k, zz].astype(F32)
            b = b + r2b[k, zz].astype(F32)
        js[zz, 0] = a
        js[zz, 1] = b
        js16[zz, 0] = a.astype(BF16)
        js16[zz, 1] = b.astype(BF16)
        return carry
    lax.fori_loop(0, 4, sum_2, 0)

    q3 = []
    for k in (4, 3, 5, 2, 6, 1, 7):
        there = (z + k) % 8
        window = pl.ds(pl.multiple_of((there % 2) * 64, 16), 80)
        q3.append(push(js16.at[there // 2, :, window], zr.at[k - 1], q3_s.at[k - 1], q3_r.at[k - 1], on_z(k)))
    for copy in q3:
        copy.wait_recv()
    total = js[zh, :, pl.ds(pl.multiple_of(zl * 64, 8), 80), :]
    for k in range(7):
        total = total + zr[k].astype(F32)
    zsum[...] = total
    fin[c, zl] = zsum[:, pl.ds(pl.multiple_of(zl * 8, 8), ROWS), :]

    q4 = [push(fin.at[c, zl], fin.at[c, zl], q4_s.at[n], q4_r.at[n], device)
          for n, device in enumerate((diagonal, partner, sibling))]
    for copy in q4:
        copy.wait_recv()

    for i in range(8):
        cols = slice(128 * i, 128 * (i + 1))
        g = fin[i // 4, i % 2, (i // 2) % 2]
        grad_ref[:, cols] = g
        next_ref[:, cols] = (1.0 - ema_rate) * anchor_ref[:, cols] + ema_rate * (
            policy_ref[:, cols] - step_size * g)

    for copy in sends:
        copy.wait_send()


def shards(inputs, cotangent, response_mask, policy, anchor):
    vmem = pl.BlockSpec(memory_space=pltpu.VMEM)
    hbm = pl.BlockSpec(memory_space=pl.ANY)
    dma = pltpu.SemaphoreType.DMA
    packed = (PACK, 128)
    scratch = [
        pltpu.VMEM((2 * LEN, D), BF16),
        pltpu.VMEM((4, 4, 4) + packed, BF16),
        pltpu.VMEM((4, 4, 4) + packed, BF16),
        pltpu.VMEM((SLAB, 256), F32),
        pltpu.VMEM((SLAB, 256), BF16),
        pltpu.VMEM((2 * LEN, HALF), F32),
        pltpu.VMEM((2 * LEN, HALF), BF16),
        pltpu.VMEM((HALF, 2 * LEN), BF16),
        pltpu.VMEM((2, 8, LEN), F32),
        pltpu.VMEM((D, HALF), F32),
        pltpu.VMEM((4, 4, 4) + packed, BF16),
        pltpu.VMEM((4, 4, 4) + packed, BF16),
        pltpu.VMEM((3, 4, 4) + packed, BF16),
        pltpu.VMEM((3, 4, 4) + packed, BF16),
        pltpu.VMEM((4, 4) + packed, F32),
        pltpu.VMEM((4, 4) + packed, F32),
        pltpu.VMEM((4, 4) + packed, BF16),
        pltpu.VMEM((4, 4) + packed, BF16),
        pltpu.VMEM((3, 4) + packed, BF16),
        pltpu.VMEM((3, 4) + packed, BF16),
        pltpu.VMEM((4, 2) + packed, F32),
        pltpu.VMEM((4, 2) + packed, BF16),
        pltpu.VMEM((7, 2, 80, 128), BF16),
        pltpu.VMEM((2, 80, 128), F32),
        pltpu.VMEM((2, 2, 2, ROWS, 128), F32),
        dma((2,)), dma((3,)), dma((3,)),
        dma((2, 3)), dma((2, 3)), dma((2, 3)), dma((2, 3)),
        dma((3,)), dma((3,)), dma((4, 3)), dma((4, 3)),
        dma((3,)), dma((3,)), dma((4, 3)), dma((4, 3)),
        dma((2, 3)), dma((2, 3)), dma((7,)), dma((7,)), dma((3,)), dma((3,)),
    ]
    return pl.pallas_call(
        kernel,
        out_shape=(jax.ShapeDtypeStruct((ROWS, KVW), F32), jax.ShapeDtypeStruct((ROWS, KVW), F32)),
        in_specs=[hbm, hbm, vmem, vmem, vmem],
        out_specs=(vmem, vmem),
        scratch_shapes=scratch,
        compiler_params=pltpu.CompilerParams(
            collective_id=0, has_side_effects=True, vmem_limit_bytes=62 * 2**20),
        cost_estimate=pl.CostEstimate(flops=4 * LEN * D * KVW, bytes_accessed=20 * 2**20, transcendentals=0),
        name="policy_step",
    )(inputs, cotangent, response_mask, policy, anchor)


def solution(mesh):
    placed = (
        P(("dp", "fsdp"), None, None),
        P(("dp", "fsdp"), None, None),
        P(("dp", "fsdp"), None),
        P("fsdp", None),
        P("fsdp", None),
    )
    return jax.shard_map(
        shards,
        mesh=mesh,
        in_specs=placed,
        out_specs=(P("fsdp", None), P("fsdp", None)),
        check_vma=False,
    )
```

time: 516 us -> 121 us (0.23)
  waiting for transfers between devices: 448 us -> 0 us
  Pallas kernels: 0 us -> 116 us
  matrix products: 24.9 us -> 0 us
  local copies, waits for them, and re-layouts: 24.5 us -> 3.39 us
  between operations: 13.8 us -> 0.64 us
    unnamed x4 -> x0, waiting for transfers between devices: 288 us -> none
    all_gather x1 -> x0, waiting for transfers between devices: 119 us -> none  [shards(): lax.all_gather(delta, 'fsdp', axis=0, tiled=True)]
    pallas_call x0 -> x1, Pallas kernels: none -> 116 us  [shards(): pl.pallas_call(kernel, out_shape=(jax.ShapeDtypeStruct((ROWS, KVW), F32),...]
    psum x1 -> x0, waiting for transfers between devices: 41.3 us -> none  [shards(): gradient = lax.psum(local_rows, 'dp')]
    dot_general x2 -> x0, matrix products: 24.9 us -> none  [the longest x1 14.3 us: shards(): jnp.dot(columns, lax.all_gather(delta, 'fsdp', axis=0, tiled=True), prefe...]
    unnamed x17 -> x2, local copies, waits for them, and re-layouts: 24.5 us -> 3.39 us
  transfers between devices with their start and end apart: 3 -> 0, of which waited for: 3 -> 0; matrix products, arithmetic and copies ran while one was open for 1% -> 0% of each run, Pallas kernels for 0% -> 0%
where the time goes in v1:
time: 121 us; the launch traced here: 120 us
  Pallas kernels  116 us (96%)
  local copies, waits for them, and re-layouts  3.39 us (3%)
    pallas_call x1, Pallas kernels, shards(): pl.pallas_call(kernel, out_shape=(jax.ShapeDtypeStruct((ROWS, KVW), F32),...  116 us
    unnamed x2, local copies, waits for them, and re-layouts  3.39 us

profile of v1, /device:TPU:1, one launch (start us, length us, event | category | flops | bytes accessed | tf_op | source)
XLA Modules:
  0.0 119.9 jit_solution(1757388865230716248)
XLA Ops:
  0.6 115.9 %policy_step.1 = (f32[72,1024]{1,0:T(8,128)}, f32[72,1024]{1,0:T(8,128)}) custom-call(bf16[1,768,4608]{2,1,0:T(8,128)(2,1)} %x_hbm.1, bf16[1,768,1024]{2,1,0:T(8,128)(2,1)} %cot_hbm.1, s32[1,768]{1,0:T(1,128)} %mask_ref.1, f32[72,1024]{1,0:T(8,128)} %policy_ref.1, f32[72,1024]{1,0:T(8,128)} %anchor_ref.1), custom_call_target="tpu_custom_call" | custom-call | flops 14495514624 | bytes 20971520 | tf_op jit(solution)/shard_map/policy_step/pallas_call | solution.py:318
  116.5 1.7 %copy.9 = f32[72,1024]{1,0:T(8,128)} copy(f32[72,1024]{1,0:T(8,128)} %get-tuple-element.4) | data formatting | bytes 589824
  118.2 1.7 %copy.10 = f32[72,1024]{1,0:T(8,128)} copy(f32[72,1024]{1,0:T(8,128)} %get-tuple-element.5) | data formatting | bytes 589824

commit v2 on v0

v2 whole, which is shorter than its diff:
```python
import jax
import jax.numpy as jnp
from jax import lax
from jax.experimental import pallas as pl
from jax.experimental.pallas import tpu as pltpu
from jax.sharding import PartitionSpec as P

kl_weight = 0.5
ema_rate = 0.01
step_size = 0.1

MESH = pl.DeviceIdType.MESH
F32 = jnp.float32
BF16 = jnp.bfloat16

LEN = 768
D = 4608
KVW = 1024
HALF = KVW // 2
WIDE = HALF // 2
ROWS = 72
SLAB = 16 * ROWS
PACK = 2 * ROWS
ORDER = (2, 1, 3, 0)
CUTS = ((64, 48, 32), (48, 64, 32))
NSEM = 200


def kernel(x_hbm, cot_hbm, mask_ref, policy_ref, anchor_ref, grad_ref, next_ref,
           xv, stage, dcol, spread, cot, sig_t, scale, g32, fin, *rest):
    lanes = [rest[17 * i:17 * (i + 1)] for i in range(2)]
    ssem, rsem, loc = rest[34:]
    dp, fs = lax.axis_index("dp"), lax.axis_index("fsdp")
    c, zl = dp % 2, dp // 2
    x, zh, y = fs // 16, (fs // 4) % 4, fs % 4
    z = zh * 2 + zl

    def at(c_, x_, y_, z_):
        return ((z_ % 2) * 2 + c_, (x_ * 4 + z_ // 2) * 4 + y_)

    def on_x(k):
        return at(c, (x + k) % 4, y, z)

    def on_y(k):
        return at(c, x, (y + k) % 4, z)

    def on_z(k):
        return at(c, x, y, (z + k) % 8)

    def on_pairs(k):
        return on_z(jnp.where(zl == 1, k, 8 - k))

    sibling = at(1 - c, x, y, z)
    partner = at(c, x, y, zh * 2 + (1 - zl))
    diagonal = at(1 - c, x, y, zh * 2 + (1 - zl))

    sends = []

    def push(src, dst, device):
        n = len(sends)
        copy = pltpu.make_async_remote_copy(
            src_ref=src, dst_ref=dst, send_sem=ssem.at[n], recv_sem=rsem.at[n],
            device_id=device, device_id_type=MESH)
        copy.start()
        sends.append(copy)
        return copy

    def arrive(copies):
        for copy in copies:
            copy.wait_recv()

    own_x = pltpu.make_async_copy(x_hbm.at[0], xv.at[pl.ds(0, LEN)], loc.at[0])
    own_x.start()
    mine = pl.multiple_of(c * HALF, HALF)
    other = pl.multiple_of((1 - c) * HALF, HALF)
    own_cot = pltpu.make_async_copy(
        cot_hbm.at[0, :, pl.ds(mine, HALF)], cot.at[pl.ds(0, LEN)], loc.at[1])
    own_cot.start()

    barrier = pltpu.get_barrier_semaphore()
    peers = [on_x(k) for k in (1, 2, 3)] + [on_y(k) for k in (1, 2, 3)]
    peers += [on_z(k) for k in range(1, 8)] + [sibling, diagonal]
    for device in peers:
        pl.semaphore_signal(barrier, inc=1, device_id=device, device_id_type=MESH)

    delta = policy_ref[...] - anchor_ref[...]
    delta = jnp.where(c == 0, delta[:, :HALF], delta[:, HALF:])
    for n, (ta, tb, tc, *_) in enumerate(lanes):
        i, j, _ = CUTS[n]
        v = jnp.concatenate([delta[:, WIDE * n:WIDE * n + 128], delta[:, WIDE * n + 128:WIDE * n + 256]], axis=0)
        ta[x, y, zh] = v[:i].astype(BF16)
        tb[y, x, zh] = v[i:i + j].astype(BF16)
        tc[zh, x, y] = v[i + j:].astype(BF16)
    weights = mask_ref[...].astype(F32)
    weights = weights / jnp.sum(weights, axis=1, keepdims=True)
    scale[0] = jnp.broadcast_to(weights, (8, LEN))

    pl.semaphore_wait(barrier, len(peers))

    first = []
    for ta, tb, tc, *_ in lanes:
        first.append([
            [push(t, t, on_pairs(k)) for k in (1, 2, 3) for t in (ta.at[x, y, zh],)],
            [push(t, t, on_pairs(k)) for k in (1, 2, 3) for t in (tb.at[y, x, zh],)],
            [push(t, t, on_y(k)) for k in (1, 2, 3) for t in (tc.at[zh, x, y],)]])

    sib = [
        push(x_hbm.at[0], xv.at[pl.ds(LEN, LEN)], sibling),
        push(cot_hbm.at[0, :, pl.ds(other, HALF)], cot.at[pl.ds(LEN, LEN)], sibling),
        push(scale.at[0], scale.at[1], sibling),
    ]

    second = []
    for n, (ta, tb, tc, *_) in enumerate(lanes):
        arrive(first[n][0])
        pa = [push(ta.at[x, y], ta.at[x, y], on_y(k)) for k in (1, 2, 3)]
        arrive(first[n][1])
        pb = [push(tb.at[y, x], tb.at[y, x], on_x(k)) for k in (1, 2, 3)]
        arrive(first[n][2])
        pc = [push(tc.at[zh, x], tc.at[zh, x], on_x(k)) for k in (1, 2, 3)]
        second.append([pa, pb, pc])

    third = []
    for n, (ta, tb, tc, *_) in enumerate(lanes):
        slabs = [[], [], [], []]
        arrive(second[n][0])
        for k in (3, 2, 1):
            slabs[4 - k].append(push(ta.at[x], ta.at[x], on_x(k)))
        arrive(second[n][1])
        arrive(second[n][2])
        for j in range(4):
            xs = (x + j) % 4
            for k in (1, 2, 3):
                slabs[j].append(push(tb.at[y, xs], tb.at[y, xs], on_y(k)))
            for k in (1, 2, 3):
                slabs[j].append(push(tc.at[zh, xs], tc.at[zh, xs], on_pairs(k)))
        third.append(slabs)

    own_x.wait()
    own_cot.wait()
    arrive(sib)

    def first_product(n, j):
        ta, tb, tc = lanes[n][:3]
        xs = (x + j) % 4
        arrive(third[n][j])

        def unpack(i, carry):
            yy, zz = i // 4, i % 4
            v = jnp.concatenate([ta[xs, yy, zz].astype(F32), tb[yy, xs, zz].astype(F32),
                                 tc[zz, xs, yy].astype(F32)], axis=0)
            row = pl.ds(pl.multiple_of(zz * 288 + yy * ROWS, 8), ROWS)
            stage[row, 0:128] = v[:ROWS]
            stage[row, 128:256] = v[ROWS:]
            return carry
        lax.fori_loop(0, 16, unpack, 0)
        dcol[...] = stage[...].astype(BF16)

        def tokens(m, carry):
            rows = pl.ds(pl.multiple_of(m * 512, 512), 512)
            lhs = xv[rows, pl.ds(pl.multiple_of(xs * SLAB, 128), SLAB)]
            out = jnp.dot(lhs, dcol[...], preferred_element_type=F32)
            spread[rows, :] = out if j == 0 else spread[rows, :] + out
            return carry
        lax.fori_loop(0, 3, tokens, 0)

    def make_signal(n):
        cols = slice(WIDE * n, WIDE * (n + 1))

        def tokens(m, carry):
            rows = pl.ds(pl.multiple_of(m * 256, 256), 256)
            u = cot[rows, cols].astype(F32) + kl_weight * spread[rows, :]
            lane = pl.ds(pl.multiple_of((m % 3) * 256, 256), 256)
            w = scale[m // 3, 0:1, lane]
            sig_t[cols, rows] = (u.T * w).astype(BF16)
            return carry
        lax.fori_loop(0, 6, tokens, 0)

    heavy = [([], [[], [], [], []], []), ([], [[], [], [], []], [])]

    def second_product(n, i):
        ga, gb, gc, ra, rb, rc = lanes[n][3:9]
        p, q, _ = CUTS[n]
        off = ORDER[i]
        xs = (x + off) % 4
        out = jnp.dot(sig_t[WIDE * n:WIDE * (n + 1), :], xv[:, pl.ds(pl.multiple_of(xs * SLAB, 128), SLAB)],
                      preferred_element_type=F32)
        stage[...] = out.T

        def pack(m, carry):
            yy, zz = m // 4, m % 4
            row = pl.ds(pl.multiple_of(zz * 288 + yy * ROWS, 8), ROWS)
            v = jnp.concatenate([stage[row, 0:128], stage[row, 128:256]], axis=0)
            g32[n, xs, zz, yy] = v
            ga[xs, yy, zz] = v[:p].astype(BF16)
            gb[yy, xs, zz] = v[p:p + q].astype(BF16)
            gc[zz, xs, yy] = v[p + q:].astype(BF16)
            return carry
        lax.fori_loop(0, 16, pack, 0)
        if off:
            heavy[n][0].append(push(ga.at[xs], ra.at[off - 1], on_x(off)))
        for k in (2, 1, 3):
            heavy[n][1][i].append(push(gb.at[(y + k) % 4, xs], rb.at[k - 1, xs], on_y(k)))
        if i == 3:
            for k in (4, 3, 5, 2, 6, 1, 7):
                there = (z + k) % 8
                window = pl.ds(pl.multiple_of((there % 2) * 16, 16), 16)
                heavy[n][2].append(push(gc.at[there // 2, :, :, window], rc.at[k - 1], on_z(k)))

    middle = [([], [], []), ([], [], [])]

    def first_sums(n):
        ra, rb, rc, ha, hb, hc, r2a, r2b, r2c = lanes[n][6:15]
        ha, ha16 = ha
        hb, hb16 = hb
        hc, hc16 = hc
        p, q, _ = CUTS[n]
        for i, off in enumerate(ORDER):
            xs = (x + off) % 4
            arrive(heavy[n][1][i])

            def sum_b(zz, carry):
                t = g32[n, xs, zz, y, p:p + q, :]
                for k in range(3):
                    t = t + rb[k, xs, zz].astype(F32)
                hb[xs, zz] = t
                hb16[xs, zz] = t.astype(BF16)
                return carry
            lax.fori_loop(0, 4, sum_b, 0)
            if off:
                middle[n][1].append(push(hb16.at[xs], r2b.at[off - 1], on_x(off)))
        arrive(heavy[n][0])
        for off in ORDER:
            yy = (y + off) % 4

            def sum_a(zz, carry):
                t = g32[n, x, zz, yy, :p, :]
                for k in range(3):
                    t = t + ra[k, yy, zz].astype(F32)
                ha[yy, zz] = t
                ha16[yy, zz] = t.astype(BF16)
                return carry
            lax.fori_loop(0, 4, sum_a, 0)
            if off:
                middle[n][0].append(push(ha16.at[yy], r2a.at[off - 1], on_y(off)))
        arrive(heavy[n][2])
        for off in ORDER:
            xs = (x + off) % 4

            def sum_c(yy, carry):
                t = g32[n, xs, zh, yy, pl.ds(pl.multiple_of(p + q + zl * 16, 8), 16), :]
                for k in range(7):
                    t = t + rc[k, xs, yy].astype(F32)
                hc[xs, yy] = t
                hc16[xs, yy] = t.astype(BF16)
                return carry
            lax.fori_loop(0, 4, sum_c, 0)
            if off:
                middle[n][2].append(push(hc16.at[xs], r2c.at[off - 1], on_x(off)))

    last = [([], []), ([], [])]

    def second_sums(n):
        (ha, _), (hb, _), (hc, _), r2a, r2b, r2c, (js, jc), (r3, r3c) = lanes[n][9:17]
        js, js16 = js
        jc, jc16 = jc
        p, q, _ = CUTS[n]
        for copies in middle[n]:
            arrive(copies)

        def sum_ab(zz, carry):
            a, b = ha[y, zz], hb[x, zz]
            for k in range(3):
                a = a + r2a[k, zz].astype(F32)
                b = b + r2b[k, zz].astype(F32)
            for side in range(2):
                s, t = (p - 32) * side, (q - 32) * side
                v = jnp.concatenate([a[s:s + 32], b[t:t + 32]], axis=0)
                js[zz, side] = v
                js16[zz, side] = v.astype(BF16)
            return carry
        lax.fori_loop(0, 4, sum_ab, 0)
        for k in (4, 3, 5, 2, 6, 1, 7):
            there = (z + k) % 8
            last[n][0].append(push(js16.at[there // 2, there % 2], r3.at[k - 1], on_z(k)))
        for yy in range(4):
            t = hc[x, yy]
            for k in range(3):
                t = t + r2c[k, yy].astype(F32)
            jc[yy] = t
            jc16[yy] = t.astype(BF16)
        for k in (2, 1, 3):
            last[n][1].append(push(jc16.at[(y + k) % 4], r3c.at[k - 1], on_y(k)))

    done = [[], []]

    def last_sums(n):
        (js, jc), (r3, r3c) = lanes[n][15:17]
        arrive(last[n][0])
        t = js[0][zh, zl]
        for k in range(7):
            t = t + r3[k].astype(F32)
        arrive(last[n][1])
        u = jc[0][y]
        for k in range(3):
            u = u + r3c[k].astype(F32)
        fin[c, zl, n] = jnp.concatenate([t, u], axis=0)
        piece = fin.at[c, zl, n]
        done[n] += [push(piece, piece, device) for device in (diagonal, partner, sibling)]

    def finish(n):
        arrive(done[n])
        p, q, _ = CUTS[n]
        for core in range(2):
            lo, hi = fin[core, 0, n], fin[core, 1, n]
            v = jnp.concatenate([lo[0:32], hi[64 - p + 32 - 32:32], lo[32:64], hi[64 - q + 32:64],
                                 lo[64:80], hi[64:80]], axis=0)
            for half in range(2):
                begin = core * HALF + n * WIDE + half * 128
                cols = slice(begin, begin + 128)
                g = v[ROWS * half:ROWS * (half + 1)]
                grad_ref[:, cols] = g
                next_ref[:, cols] = (1.0 - ema_rate) * anchor_ref[:, cols] + ema_rate * (
                    policy_ref[:, cols] - step_size * g)

    for j in range(4):
        first_product(0, j)
    make_signal(0)
    for i in range(4):
        second_product(0, i)
    for j in range(4):
        first_product(1, j)
    make_signal(1)
    for i in range(3):
        second_product(1, i)
    first_sums(0)
    second_product(1, 3)
    second_sums(0)
    first_sums(1)
    last_sums(0)
    second_sums(1)
    finish(0)
    last_sums(1)
    finish(1)

    for copy in sends:
        copy.wait_send()


def shards(inputs, cotangent, response_mask, policy, anchor):
    vmem = pl.BlockSpec(memory_space=pltpu.VMEM)
    hbm = pl.BlockSpec(memory_space=pl.ANY)
    scratch = [
        pltpu.VMEM((2 * LEN, D), BF16),
        pltpu.VMEM((SLAB, WIDE), F32),
        pltpu.VMEM((SLAB, WIDE), BF16),
        pltpu.VMEM((2 * LEN, WIDE), F32),
        pltpu.VMEM((2 * LEN, HALF), BF16),
        pltpu.VMEM((HALF, 2 * LEN), BF16),
        pltpu.VMEM((2, 8, LEN), F32),
        pltpu.VMEM((2, 4, 4, 4, PACK, 128), F32),
        pltpu.VMEM((2, 2, 2, 80, 128), F32),
    ]
    for p, q, r in CUTS:
        scratch += [pltpu.VMEM((4, 4, 4, m, 128), BF16) for m in (p, q, r)]
        scratch += [pltpu.VMEM((4, 4, 4, m, 128), BF16) for m in (p, q, r)]
        scratch += [pltpu.VMEM((3, 4, 4, m, 128), BF16) for m in (p, q)]
        scratch += [pltpu.VMEM((7, 4, 4, 16, 128), BF16)]
        scratch += [(pltpu.VMEM((4, 4, m, 128), F32), pltpu.VMEM((4, 4, m, 128), BF16))
                    for m in (p, q, 16)]
        scratch += [pltpu.VMEM((3, 4, m, 128), BF16) for m in (p, q, 16)]
        scratch += [((pltpu.VMEM((4, 2, 64, 128), F32), pltpu.VMEM((4, 2, 64, 128), BF16)),
                     (pltpu.VMEM((4, 16, 128), F32), pltpu.VMEM((4, 16, 128), BF16)))]
        scratch += [(pltpu.VMEM((7, 64, 128), BF16), pltpu.VMEM((3, 16, 128), BF16))]
    scratch += [pltpu.SemaphoreType.DMA((NSEM,)), pltpu.SemaphoreType.DMA((NSEM,)),
                pltpu.SemaphoreType.DMA((2,))]
    return pl.pallas_call(
        kernel,
        out_shape=(jax.ShapeDtypeStruct((ROWS, KVW), F32), jax.ShapeDtypeStruct((ROWS, KVW), F32)),
        in_specs=[hbm, hbm, vmem, vmem, vmem],
        out_specs=(vmem, vmem),
        scratch_shapes=scratch,
        compiler_params=pltpu.CompilerParams(
            collective_id=0, has_side_effects=True, vmem_limit_bytes=62 * 2**20),
        cost_estimate=pl.CostEstimate(flops=4 * LEN * D * KVW, bytes_accessed=20 * 2**20, transcendentals=0),
        name="policy_step",
    )(inputs, cotangent, response_mask, policy, anchor)


def solution(mesh):
    placed = (
        P(("dp", "fsdp"), None, None),
        P(("dp", "fsdp"), None, None),
        P(("dp", "fsdp"), None),
        P("fsdp", None),
        P("fsdp", None),
    )
    return jax.shard_map(
        shards,
        mesh=mesh,
        in_specs=placed,
        out_specs=(P("fsdp", None), P("fsdp", None)),
        check_vma=False,
    )
```

time: 516 us -> 97 us (0.19)
  waiting for transfers between devices: 448 us -> 0 us
  Pallas kernels: 0 us -> 91.3 us
  matrix products: 24.9 us -> 0 us
  local copies, waits for them, and re-layouts: 24.5 us -> 3.39 us
  between operations: 13.8 us -> 0.64 us
    unnamed x4 -> x0, waiting for transfers between devices: 288 us -> none
    all_gather x1 -> x0, waiting for transfers between devices: 119 us -> none  [shards(): lax.all_gather(delta, 'fsdp', axis=0, tiled=True)]
    pallas_call x0 -> x1, Pallas kernels: none -> 91.3 us  [shards(): pl.pallas_call(kernel, out_shape=(jax.ShapeDtypeStruct((ROWS, KVW), F32),...]
    psum x1 -> x0, waiting for transfers between devices: 41.3 us -> none  [shards(): gradient = lax.psum(local_rows, 'dp')]
    dot_general x2 -> x0, matrix products: 24.9 us -> none  [the longest x1 14.3 us: shards(): jnp.dot(columns, lax.all_gather(delta, 'fsdp', axis=0, tiled=True), prefe...]
    unnamed x17 -> x2, local copies, waits for them, and re-layouts: 24.5 us -> 3.39 us
  transfers between devices with their start and end apart: 3 -> 0, of which waited for: 3 -> 0; matrix products, arithmetic and copies ran while one was open for 1% -> 0% of each run, Pallas kernels for 0% -> 0%
where the time goes in v2:
time: 97 us; the launch traced here: 95.3 us
  Pallas kernels  91.3 us (94%)
  local copies, waits for them, and re-layouts  3.39 us (3%)
    pallas_call x1, Pallas kernels, shards(): pl.pallas_call(kernel, out_shape=(jax.ShapeDtypeStruct((ROWS, KVW), F32),...  91.3 us
    unnamed x2, local copies, waits for them, and re-layouts  3.39 us

profile of v2, /device:TPU:1, one launch (start us, length us, event | category | flops | bytes accessed | tf_op | source)
XLA Modules:
  0.0 95.3 jit_solution(1382263918515806785)
XLA Ops:
  0.6 91.3 %policy_step.1 = (f32[72,1024]{1,0:T(8,128)}, f32[72,1024]{1,0:T(8,128)}) custom-call(bf16[1,768,4608]{2,1,0:T(8,128)(2,1)} %x_hbm.1, bf16[1,768,1024]{2,1,0:T(8,128)(2,1)} %cot_hbm.1, s32[1,768]{1,0:T(1,128)} %mask_ref.1, f32[72,1024]{1,0:T(8,128)} %policy_ref.1, f32[72,1024]{1,0:T(8,128)} %anchor_ref.1), custom_call_target="tpu_custom_call" | custom-call | flops 14495514624 | bytes 20971520 | tf_op jit(solution)/shard_map/policy_step/pallas_call | solution.py:377
  91.9 1.7 %copy.9 = f32[72,1024]{1,0:T(8,128)} copy(f32[72,1024]{1,0:T(8,128)} %get-tuple-element.4) | data formatting | bytes 589824
  93.6 1.7 %copy.10 = f32[72,1024]{1,0:T(8,128)} copy(f32[72,1024]{1,0:T(8,128)} %get-tuple-element.5) | data formatting | bytes 589824

commit v3 on v2

v3 whole, which is shorter than its diff:
```python
import jax
import jax.numpy as jnp
from jax import lax
from jax.experimental import pallas as pl
from jax.experimental.pallas import tpu as pltpu
from jax.sharding import PartitionSpec as P

kl_weight = 0.5
ema_rate = 0.01
step_size = 0.1

MESH = pl.DeviceIdType.MESH
F32 = jnp.float32
BF16 = jnp.bfloat16

LEN = 768
D = 4608
KVW = 1024
HALF = KVW // 2
WIDE = HALF // 2
ROWS = 72
SLAB = 16 * ROWS
PACK = 2 * ROWS
CUTS = ((64, 48, 32), (48, 64, 32))
NSEM = 61


def kernel(x_hbm, cot_hbm, mask_ref, policy_ref, anchor_ref, grad_ref, next_ref,
           xv, stage, dcol, spread, cot, sig_t, scale, g32, fin, *rest):
    lanes = [rest[17 * i:17 * (i + 1)] for i in range(2)]
    ssem, rsem, loc = rest[34:]
    dp, fs = lax.axis_index("dp"), lax.axis_index("fsdp")
    c, zl = dp % 2, dp // 2
    x, zh, y = fs // 16, (fs // 4) % 4, fs % 4
    z = zh * 2 + zl

    def at(c_, x_, y_, z_):
        return ((z_ % 2) * 2 + c_, (x_ * 4 + z_ // 2) * 4 + y_)

    def on_x(k):
        return at(c, (x + k) % 4, y, z)

    def on_y(k):
        return at(c, x, (y + k) % 4, z)

    def on_z(k):
        return at(c, x, y, (z + k) % 8)

    def on_pairs(k):
        return on_z(jnp.where(zl == 1, k, 8 - k))

    sibling = at(1 - c, x, y, z)
    partner = at(c, x, y, zh * 2 + (1 - zl))
    diagonal = at(1 - c, x, y, zh * 2 + (1 - zl))

    groups = []

    class Group:
        def __init__(self, span):
            self.span, self.n = span, len(groups)
            groups.append(self)

        def push(self, src, dst, device):
            pltpu.make_async_remote_copy(
                src_ref=src, dst_ref=dst, send_sem=ssem.at[self.n], recv_sem=rsem.at[self.n],
                device_id=device, device_id_type=MESH).start()

        def arrive(self):
            pltpu.make_async_copy(self.span, self.span, rsem.at[self.n]).wait()

        def sent(self):
            pltpu.make_async_copy(self.span, self.span, ssem.at[self.n]).wait()

    def spread_out(span, ref, targets):
        group = Group(span)
        for device in targets:
            group.push(ref, ref, device)
        return group

    def planar(n, xs, yy):
        return (yy, xs) if n else (xs, yy)

    on_slow, on_fast = (on_x, on_y), (on_y, on_x)

    own_x = pltpu.make_async_copy(x_hbm.at[0], xv.at[pl.ds(0, LEN)], loc.at[0])
    own_x.start()
    mine = pl.multiple_of(c * HALF, HALF)
    other = pl.multiple_of((1 - c) * HALF, HALF)
    own_cot = pltpu.make_async_copy(
        cot_hbm.at[0, :, pl.ds(mine, HALF)], cot.at[pl.ds(0, LEN)], loc.at[1])
    own_cot.start()

    barrier = pltpu.get_barrier_semaphore()
    peers = [on_x(k) for k in (1, 2, 3)] + [on_y(k) for k in (1, 2, 3)]
    peers += [on_z(k) for k in range(1, 8)] + [sibling, diagonal]
    for device in peers:
        pl.semaphore_signal(barrier, inc=1, device_id=device, device_id_type=MESH)

    delta = policy_ref[...] - anchor_ref[...]
    delta = jnp.where(c == 0, delta[:, :HALF], delta[:, HALF:])
    for n, (ta, tb, tc, *_) in enumerate(lanes):
        p, q, _ = CUTS[n]
        v = jnp.concatenate([delta[:, WIDE * n:WIDE * n + 128], delta[:, WIDE * n + 128:WIDE * n + 256]], axis=0)
        ta[x, y, zh] = v[:p].astype(BF16)
        tb[y, x, zh] = v[p:p + q].astype(BF16)
        tc[(zh, *planar(n, x, y))] = v[p + q:].astype(BF16)
    weights = mask_ref[...].astype(F32)
    weights = weights / jnp.sum(weights, axis=1, keepdims=True)
    scale[0] = jnp.broadcast_to(weights, (8, LEN))

    pl.semaphore_wait(barrier, len(peers))

    three = pl.ds(0, 3)
    first = []
    for n, (ta, tb, tc, *_) in enumerate(lanes):
        first.append([
            spread_out(ta.at[0, 0, three], ta.at[x, y, zh], [on_pairs(k) for k in (1, 2, 3)]),
            spread_out(tb.at[0, 0, three], tb.at[y, x, zh], [on_pairs(k) for k in (1, 2, 3)]),
            spread_out(tc.at[0, 0, three], tc.at[(zh, *planar(n, x, y))],
                       [on_fast[n](k) for k in (1, 2, 3)])])

    sib = [Group(xv.at[pl.ds(LEN, LEN)]), Group(cot.at[pl.ds(LEN, LEN)]), Group(scale.at[1])]
    sib[0].push(x_hbm.at[0], xv.at[pl.ds(LEN, LEN)], sibling)
    sib[1].push(cot_hbm.at[0, :, pl.ds(other, HALF)], cot.at[pl.ds(LEN, LEN)], sibling)
    sib[2].push(scale.at[0], scale.at[1], sibling)

    second = []
    for n, (ta, tb, tc, *_) in enumerate(lanes):
        first[n][0].arrive()
        pa = spread_out(ta.at[0, three], ta.at[x, y], [on_y(k) for k in (1, 2, 3)])
        first[n][1].arrive()
        pb = spread_out(tb.at[0, three], tb.at[y, x], [on_x(k) for k in (1, 2, 3)])
        first[n][2].arrive()
        pc = spread_out(tc.at[0, three], tc.at[zh, planar(n, x, y)[0]], [on_slow[n](k) for k in (1, 2, 3)])
        second.append([pa, pb, pc])

    front, back = pl.ds(0, 2), pl.ds(2, 2)

    def ring_start(t, me, on):
        one, two = Group(t.at[0]), Group(t.at[0])
        for group, rows, k in ((one, front, 1), (one, back, 3), (two, back, 1), (two, front, 3)):
            group.push(t.at[me, rows], t.at[me, rows], on(k))
        return one, two

    def ring_forward(t, me, on, started):
        started[0].arrive()
        group = Group(t.at[0])
        for owner, rows, k in (((me + 3) % 4, front, 1), ((me + 1) % 4, back, 3)):
            group.push(t.at[owner, rows], t.at[owner, rows], on(k))
        return started[1], group

    def third_start(n):
        ta, tb, tc = lanes[n][:3]
        second[n][0].arrive()
        a = ring_start(ta, x, on_x)
        second[n][1].arrive()
        b = ring_start(tb, y, on_y)
        second[n][2].arrive()
        c1 = [spread_out(tc.at[0, half], tc.at[zh, half], [on_pairs(1)]) for half in (front, back)]
        return a, b, c1

    def third_forward(n, started):
        ta, tb, tc = lanes[n][:3]
        a, b, c1 = started
        a = ring_forward(ta, x, on_x, a)
        b = ring_forward(tb, y, on_y, b)
        relay = Group(tc.at[pl.ds(0, 2)])
        owner = (zh + jnp.where(zl == 1, 1, 3)) % 4
        for group, half in zip(c1, (front, back)):
            group.arrive()
            for k in (1, 2):
                relay.push(tc.at[owner, half], tc.at[owner, half], on_z(jnp.where(zl == 1, 8 - k, k)))
        return (*a, *b, relay)

    def first_product(n):
        ta, tb, tc = lanes[n][:3]
        for xs in range(4):
            def unpack(i, carry):
                yy, zz = i // 4, i % 4
                v = jnp.concatenate([ta[xs, yy, zz].astype(F32), tb[yy, xs, zz].astype(F32),
                                     tc[(zz, *planar(n, xs, yy))].astype(F32)], axis=0)
                row = pl.ds(pl.multiple_of(zz * 288 + yy * ROWS, 8), ROWS)
                stage[row, 0:128] = v[:ROWS]
                stage[row, 128:256] = v[ROWS:]
                return carry
            lax.fori_loop(0, 16, unpack, 0)
            dcol[SLAB * xs:SLAB * (xs + 1), :] = stage[...].astype(BF16)

        def tokens(m):
            rows = pl.ds(m * LEN, LEN)
            spread[rows, :] = jnp.dot(xv[rows, :], dcol[...], preferred_element_type=F32)
        tokens(0)
        tokens(1)

    def make_signal(n):
        cols = slice(WIDE * n, WIDE * (n + 1))

        def tokens(m, carry):
            rows = pl.ds(pl.multiple_of(m * 256, 256), 256)
            u = cot[rows, cols].astype(F32) + kl_weight * spread[rows, :]
            lane = pl.ds(pl.multiple_of((m % 3) * 256, 256), 256)
            w = scale[m // 3, 0:1, lane]
            sig_t[cols, rows] = (u.T * w).astype(BF16)
            return carry
        lax.fori_loop(0, 6, tokens, 0)

    near = jnp.where(x % 2 == 0, 1, 3)
    order = (2, 4 - near, near, 0)
    heavy = [[None, [], None], [None, [], None]]

    def second_product(n, i):
        ga, gb, gc, ra, rb, rc = lanes[n][3:9]
        p, q, _ = CUTS[n]
        off = order[i]
        xs = (x + off) % 4
        out = jnp.dot(sig_t[WIDE * n:WIDE * (n + 1), :], xv[:, pl.ds(pl.multiple_of(xs * SLAB, 128), SLAB)],
                      preferred_element_type=F32)
        stage[...] = out.T

        def pack(m, carry):
            yy, zz = m // 4, m % 4
            row = pl.ds(pl.multiple_of(zz * 288 + yy * ROWS, 8), ROWS)
            v = jnp.concatenate([stage[row, 0:128], stage[row, 128:256]], axis=0)
            g32[n, xs, zz, yy] = v
            ga[xs, yy, zz] = v[:p].astype(BF16)
            gb[yy, xs, zz] = v[p:p + q].astype(BF16)
            gc[(zz, *planar(n, xs, yy))] = v[p + q:].astype(BF16)
            return carry
        lax.fori_loop(0, 16, pack, 0)
        if i == 0:
            heavy[n][0], heavy[n][2] = Group(ra), Group(rc)
        if i < 3:
            heavy[n][0].push(ga.at[xs], ra.at[off - 1], on_x(off))
        heavy[n][1].append(Group(rb.at[:, 0]))
        for k in (2, 1, 3):
            heavy[n][1][i].push(gb.at[(y + k) % 4, xs], rb.at[k - 1, xs], on_y(k))
        if i % 2:
            pair = pl.ds((xs // 2) * 2, 2)
            for k in (4, 3, 5, 2, 6, 1, 7):
                there = (z + k) % 8
                window = pl.ds(pl.multiple_of((there % 2) * 16, 16), 16)
                if n:
                    heavy[n][2].push(gc.at[there // 2, :, pair, window], rc.at[k - 1, :, pair], on_z(k))
                else:
                    heavy[n][2].push(gc.at[there // 2, pair, :, window], rc.at[k - 1, pair], on_z(k))

    middle = [None, None]

    def first_sums(n):
        ra, rb, rc, ha, hb, hc, r2a, r2b, r2c = lanes[n][6:15]
        ha, ha16 = ha
        hb, hb16 = hb
        hc, hc16 = hc
        p, q, _ = CUTS[n]
        middle[n] = [Group(r2a), Group(r2b), Group(r2c)]
        for i, off in enumerate(order):
            xs = (x + off) % 4
            heavy[n][1][i].arrive()

            def sum_b(zz, carry):
                t = g32[n, xs, zz, y, p:p + q, :]
                for k in range(3):
                    t = t + rb[k, xs, zz].astype(F32)
                hb[xs, zz] = t
                hb16[xs, zz] = t.astype(BF16)
                return carry
            lax.fori_loop(0, 4, sum_b, 0)
            if i < 3:
                middle[n][1].push(hb16.at[xs], r2b.at[off - 1], on_x(off))
        heavy[n][0].arrive()
        for off in (2, 1, 3, 0):
            yy = (y + off) % 4

            def sum_a(zz, carry):
                t = g32[n, x, zz, yy, :p, :]
                for k in range(3):
                    t = t + ra[k, yy, zz].astype(F32)
                ha[yy, zz] = t
                ha16[yy, zz] = t.astype(BF16)
                return carry
            lax.fori_loop(0, 4, sum_a, 0)
            if off:
                middle[n][0].push(ha16.at[yy], r2a.at[off - 1], on_y(off))
        heavy[n][2].arrive()
        for off in (2, 1, 3, 0):
            slow = (planar(n, x, y)[0] + off) % 4

            def sum_c(fast, carry):
                xs, yy = planar(n, slow, fast)
                t = g32[n, xs, zh, yy, pl.ds(pl.multiple_of(p + q + zl * 16, 8), 16), :]
                for k in range(7):
                    t = t + rc[k, slow, fast].astype(F32)
                hc[slow, fast] = t
                hc16[slow, fast] = t.astype(BF16)
                return carry
            lax.fori_loop(0, 4, sum_c, 0)
            if off:
                middle[n][2].push(hc16.at[slow], r2c.at[off - 1], on_slow[n](off))

    last = [None, None]

    def second_sums(n):
        (ha, _), (hb, _), (hc, _), r2a, r2b, r2c, (js, jc), (r3, r3c) = lanes[n][9:17]
        js, js16 = js
        jc, jc16 = jc
        p, q, _ = CUTS[n]
        last[n] = [Group(r3), Group(r3c)]
        for group in middle[n]:
            group.arrive()

        def sum_ab(zz, carry):
            a, b = ha[y, zz], hb[x, zz]
            for k in range(3):
                a = a + r2a[k, zz].astype(F32)
                b = b + r2b[k, zz].astype(F32)
            for side in range(2):
                s, t = (p - 32) * side, (q - 32) * side
                v = jnp.concatenate([a[s:s + 32], b[t:t + 32]], axis=0)
                js[zz, side] = v
                js16[zz, side] = v.astype(BF16)
            return carry
        lax.fori_loop(0, 4, sum_ab, 0)
        for k in (4, 3, 5, 2, 6, 1, 7):
            there = (z + k) % 8
            last[n][0].push(js16.at[there // 2, there % 2], r3.at[k - 1], on_z(k))
        slow, fast = planar(n, x, y)
        for there in range(4):
            t = hc[slow, there]
            for k in range(3):
                t = t + r2c[k, there].astype(F32)
            jc[there] = t
            jc16[there] = t.astype(BF16)
        for k in (2, 1, 3):
            last[n][1].push(jc16.at[(fast + k) % 4], r3c.at[k - 1], on_fast[n](k))

    done = [None, None]

    def last_sums(n):
        (js, jc), (r3, r3c) = lanes[n][15:17]
        last[n][0].arrive()
        t = js[0][zh, zl]
        for k in range(7):
            t = t + r3[k].astype(F32)
        last[n][1].arrive()
        u = jc[0][planar(n, x, y)[1]]
        for k in range(3):
            u = u + r3c[k].astype(F32)
        fin[n, c * 2 + zl] = jnp.concatenate([t, u], axis=0)
        done[n] = spread_out(fin.at[0, three], fin.at[n, c * 2 + zl], (diagonal, partner, sibling))

    def finish(n):
        done[n].arrive()
        p, q, _ = CUTS[n]
        for core in range(2):
            lo, hi = fin[n, core * 2], fin[n, core * 2 + 1]
            v = jnp.concatenate([lo[0:32], hi[64 - p + 32 - 32:32], lo[32:64], hi[64 - q + 32:64],
                                 lo[64:80], hi[64:80]], axis=0)
            for half in range(2):
                begin = core * HALF + n * WIDE + half * 128
                cols = slice(begin, begin + 128)
                g = v[ROWS * half:ROWS * (half + 1)]
                grad_ref[:, cols] = g
                next_ref[:, cols] = (1.0 - ema_rate) * anchor_ref[:, cols] + ema_rate * (
                    policy_ref[:, cols] - step_size * g)

    started = third_start(0)
    rest0 = third_forward(0, started)
    started = third_start(1)
    own_x.wait()
    own_cot.wait()
    for group in sib:
        group.arrive()
    for group in rest0:
        group.arrive()
    first_product(0)
    rest1 = third_forward(1, started)
    make_signal(0)
    for i in range(4):
        second_product(0, i)
    for group in rest1:
        group.arrive()
    first_product(1)
    make_signal(1)
    for i in range(3):
        second_product(1, i)
    first_sums(0)
    second_product(1, 3)
    second_sums(0)
    first_sums(1)
    last_sums(0)
    second_sums(1)
    finish(0)
    last_sums(1)
    finish(1)

    for group in groups:
        group.sent()


def shards(inputs, cotangent, response_mask, policy, anchor):
    vmem = pl.BlockSpec(memory_space=pltpu.VMEM)
    hbm = pl.BlockSpec(memory_space=pl.ANY)
    scratch = [
        pltpu.VMEM((2 * LEN, D), BF16),
        pltpu.VMEM((SLAB, WIDE), F32),
        pltpu.VMEM((D, WIDE), BF16),
        pltpu.VMEM((2 * LEN, WIDE), F32),
        pltpu.VMEM((2 * LEN, HALF), BF16),
        pltpu.VMEM((HALF, 2 * LEN), BF16),
        pltpu.VMEM((2, 8, LEN), F32),
        pltpu.VMEM((2, 4, 4, 4, PACK, 128), F32),
        pltpu.VMEM((2, 4, 80, 128), F32),
    ]
    for p, q, r in CUTS:
        scratch += [pltpu.VMEM((4, 4, 4, m, 128), BF16) for m in (p, q, r)]
        scratch += [pltpu.VMEM((4, 4, 4, m, 128), BF16) for m in (p, q, r)]
        scratch += [pltpu.VMEM((3, 4, 4, m, 128), BF16) for m in (p, q)]
        scratch += [pltpu.VMEM((7, 4, 4, 16, 128), BF16)]
        scratch += [(pltpu.VMEM((4, 4, m, 128), F32), pltpu.VMEM((4, 4, m, 128), BF16))
                    for m in (p, q, 16)]
        scratch += [pltpu.VMEM((3, 4, m, 128), BF16) for m in (p, q, 16)]
        scratch += [((pltpu.VMEM((4, 2, 64, 128), F32), pltpu.VMEM((4, 2, 64, 128), BF16)),
                     (pltpu.VMEM((4, 16, 128), F32), pltpu.VMEM((4, 16, 128), BF16)))]
        scratch += [(pltpu.VMEM((7, 64, 128), BF16), pltpu.VMEM((3, 16, 128), BF16))]
    scratch += [pltpu.SemaphoreType.DMA((NSEM,)), pltpu.SemaphoreType.DMA((NSEM,)),
                pltpu.SemaphoreType.DMA((2,))]
    rows = jax.ShapeDtypeStruct((ROWS, KVW), F32)
    return pl.pallas_call(
        kernel,
        out_shape=(rows, rows),
        in_specs=[hbm, hbm, vmem, vmem, vmem],
        out_specs=(vmem, vmem),
        scratch_shapes=scratch,
        compiler_params=pltpu.CompilerParams(
            collective_id=0, has_side_effects=True, vmem_limit_bytes=62 * 2**20),
        cost_estimate=pl.CostEstimate(flops=4 * LEN * D * KVW, bytes_accessed=20 * 2**20, transcendentals=0),
        name="policy_step",
    )(inputs, cotangent, response_mask, policy, anchor)


def solution(mesh):
    placed = (
        P(("dp", "fsdp"), None, None),
        P(("dp", "fsdp"), None, None),
        P(("dp", "fsdp"), None),
        P("fsdp", None),
        P("fsdp", None),
    )
    return jax.shard_map(
        shards,
        mesh=mesh,
        in_specs=placed,
        out_specs=(P("fsdp", None), P("fsdp", None)),
        check_vma=False,
    )
```

time: 97 us -> 90.4 us (0.932); the launches traced: 95.3 us -> 90.2 us
  Pallas kernels: 91.3 us -> 86.2 us
    pallas_call x1, Pallas kernels: 91.3 us -> 86.2 us  [shards(): pl.pallas_call(kernel, out_shape=(rows, rows), in_specs=[hbm, hbm, vmem,...]
where the time goes in v3:
time: 90.4 us; the launch traced here: 90.2 us
  Pallas kernels  86.2 us (95%)
  local copies, waits for them, and re-layouts  3.39 us (4%)
    pallas_call x1, Pallas kernels, shards(): pl.pallas_call(kernel, out_shape=(rows, rows), in_specs=[hbm, hbm, vmem,...  86.2 us
    unnamed x2, local copies, waits for them, and re-layouts  3.39 us

profile of v3, /device:TPU:1, one launch (start us, length us, event | category | flops | bytes accessed | tf_op | source)
XLA Modules:
  0.0 90.2 jit_solution(4456973553715963232)
XLA Ops:
  0.6 86.2 %policy_step.1 = (f32[72,1024]{1,0:T(8,128)}, f32[72,1024]{1,0:T(8,128)}) custom-call(bf16[1,768,4608]{2,1,0:T(8,128)(2,1)} %x_hbm.1, bf16[1,768,1024]{2,1,0:T(8,128)(2,1)} %cot_hbm.1, s32[1,768]{1,0:T(1,128)} %mask_ref.1, f32[72,1024]{1,0:T(8,128)} %policy_ref.1, f32[72,1024]{1,0:T(8,128)} %anchor_ref.1), custom_call_target="tpu_custom_call" | custom-call | flops 14495514624 | bytes 20971520 | tf_op jit(solution)/shard_map/policy_step/pallas_call | solution.py:428
  86.9 1.7 %copy.9 = f32[72,1024]{1,0:T(8,128)} copy(f32[72,1024]{1,0:T(8,128)} %get-tuple-element.4) | data formatting | bytes 589824
  88.5 1.7 %copy.10 = f32[72,1024]{1,0:T(8,128)} copy(f32[72,1024]{1,0:T(8,128)} %get-tuple-element.5) | data formatting | bytes 589824

commit v4 on v3

--- a/solution.py
+++ b/solution.py
@@ -22,11 +22,12 @@
 SLAB = 16 * ROWS
 PACK = 2 * ROWS
 CUTS = ((64, 48, 32), (48, 64, 32))
-NSEM = 61
-
-
-def kernel(x_hbm, cot_hbm, mask_ref, policy_ref, anchor_ref, grad_ref, next_ref,
-           xv, stage, dcol, spread, cot, sig_t, scale, g32, fin, *rest):
+AG = ((64, 64, 16), (64, 64, 16))
+NSEM = 64
+
+
+def kernel(x_hbm, cot_hbm, mask_hbm, policy_hbm, anchor_hbm, grad_ref, next_ref,
+           mask_ref, policy_ref, anchor_ref, xv, stage, dcol, spread, cot, sig_t, scale, g32, fin, *rest):
     lanes = [rest[17 * i:17 * (i + 1)] for i in range(2)]
     ssem, rsem, loc = rest[34:]
     dp, fs = lax.axis_index("dp"), lax.axis_index("fsdp")
@@ -78,10 +79,14 @@
         return group
 
     def planar(n, xs, yy):
-        return (yy, xs) if n else (xs, yy)
-
-    on_slow, on_fast = (on_x, on_y), (on_y, on_x)
-
+        return (xs, yy) if n else (yy, xs)
+
+    on_slow, on_fast = (on_y, on_x), (on_x, on_y)
+
+    small = [pltpu.make_async_copy(src, dst, loc.at[2 + n]) for n, (src, dst) in enumerate((
+        (policy_hbm, policy_ref), (anchor_hbm, anchor_ref), (mask_hbm, mask_ref)))]
+    for copy in small:
+        copy.start()
     own_x = pltpu.make_async_copy(x_hbm.at[0], xv.at[pl.ds(0, LEN)], loc.at[0])
     own_x.start()
     mine = pl.multiple_of(c * HALF, HALF)
@@ -96,10 +101,12 @@
     for device in peers:
         pl.semaphore_signal(barrier, inc=1, device_id=device, device_id_type=MESH)
 
+    for copy in small:
+        copy.wait()
     delta = policy_ref[...] - anchor_ref[...]
     delta = jnp.where(c == 0, delta[:, :HALF], delta[:, HALF:])
     for n, (ta, tb, tc, *_) in enumerate(lanes):
-        p, q, _ = CUTS[n]
+        p, q, _ = AG[n]
         v = jnp.concatenate([delta[:, WIDE * n:WIDE * n + 128], delta[:, WIDE * n + 128:WIDE * n + 256]], axis=0)
         ta[x, y, zh] = v[:p].astype(BF16)
         tb[y, x, zh] = v[p:p + q].astype(BF16)
@@ -124,15 +131,15 @@
     sib[1].push(cot_hbm.at[0, :, pl.ds(other, HALF)], cot.at[pl.ds(LEN, LEN)], sibling)
     sib[2].push(scale.at[0], scale.at[1], sibling)
 
-    second = []
-    for n, (ta, tb, tc, *_) in enumerate(lanes):
+    def second_start(n):
+        ta, tb, tc = lanes[n][:3]
         first[n][0].arrive()
         pa = spread_out(ta.at[0, three], ta.at[x, y], [on_y(k) for k in (1, 2, 3)])
         first[n][1].arrive()
         pb = spread_out(tb.at[0, three], tb.at[y, x], [on_x(k) for k in (1, 2, 3)])
         first[n][2].arrive()
         pc = spread_out(tc.at[0, three], tc.at[zh, planar(n, x, y)[0]], [on_slow[n](k) for k in (1, 2, 3)])
-        second.append([pa, pb, pc])
+        return pa, pb, pc
 
     front, back = pl.ds(0, 2), pl.ds(2, 2)
 
@@ -149,13 +156,13 @@
             group.push(t.at[owner, rows], t.at[owner, rows], on(k))
         return started[1], group
 
-    def third_start(n):
+    def third_start(n, second):
         ta, tb, tc = lanes[n][:3]
-        second[n][0].arrive()
+        second[0].arrive()
         a = ring_start(ta, x, on_x)
-        second[n][1].arrive()
+        second[1].arrive()
         b = ring_start(tb, y, on_y)
-        second[n][2].arrive()
+        second[2].arrive()
         c1 = [spread_out(tc.at[0, half], tc.at[zh, half], [on_pairs(1)]) for half in (front, back)]
         return a, b, c1
 
@@ -228,21 +235,21 @@
             return carry
         lax.fori_loop(0, 16, pack, 0)
         if i == 0:
-            heavy[n][0], heavy[n][2] = Group(ra), Group(rc)
+            heavy[n][0], heavy[n][2] = Group(ra), [] if n else [Group(rc)]
         if i < 3:
             heavy[n][0].push(ga.at[xs], ra.at[off - 1], on_x(off))
         heavy[n][1].append(Group(rb.at[:, 0]))
         for k in (2, 1, 3):
             heavy[n][1][i].push(gb.at[(y + k) % 4, xs], rb.at[k - 1, xs], on_y(k))
-        if i % 2:
-            pair = pl.ds((xs // 2) * 2, 2)
-            for k in (4, 3, 5, 2, 6, 1, 7):
-                there = (z + k) % 8
-                window = pl.ds(pl.multiple_of((there % 2) * 16, 16), 16)
-                if n:
-                    heavy[n][2].push(gc.at[there // 2, :, pair, window], rc.at[k - 1, :, pair], on_z(k))
-                else:
-                    heavy[n][2].push(gc.at[there // 2, pair, :, window], rc.at[k - 1, pair], on_z(k))
+        if n:
+            heavy[n][2].append(Group(rc.at[:, 0]))
+        for k in (4, 3, 5, 2, 6, 1, 7):
+            there = (z + k) % 8
+            window = pl.ds(pl.multiple_of((there % 2) * 16, 16), 16)
+            if n:
+                heavy[n][2][i].push(gc.at[there // 2, xs, :, window], rc.at[k - 1, xs], on_z(k))
+            else:
+                heavy[n][2][0].push(gc.at[there // 2, :, xs, window], rc.at[k - 1, :, xs], on_z(k))
 
     middle = [None, None]
 
@@ -253,8 +260,9 @@
         hc, hc16 = hc
         p, q, _ = CUTS[n]
         middle[n] = [Group(r2a), Group(r2b), Group(r2c)]
-        for i, off in enumerate(order):
-            xs = (x + off) % 4
+
+        def part_b(i):
+            xs = (x + order[i]) % 4
             heavy[n][1][i].arrive()
 
             def sum_b(zz, carry):
@@ -266,24 +274,28 @@
                 return carry
             lax.fori_loop(0, 4, sum_b, 0)
             if i < 3:
-                middle[n][1].push(hb16.at[xs], r2b.at[off - 1], on_x(off))
-        heavy[n][0].arrive()
-        for off in (2, 1, 3, 0):
-            yy = (y + off) % 4
-
-            def sum_a(zz, carry):
-                t = g32[n, x, zz, yy, :p, :]
-                for k in range(3):
-                    t = t + ra[k, yy, zz].astype(F32)
-                ha[yy, zz] = t
-                ha16[yy, zz] = t.astype(BF16)
-                return carry
-            lax.fori_loop(0, 4, sum_a, 0)
-            if off:
-                middle[n][0].push(ha16.at[yy], r2a.at[off - 1], on_y(off))
-        heavy[n][2].arrive()
-        for off in (2, 1, 3, 0):
-            slow = (planar(n, x, y)[0] + off) % 4
+                middle[n][1].push(hb16.at[xs], r2b.at[order[i] - 1], on_x(order[i]))
+
+        def part_a():
+            heavy[n][0].arrive()
+            for off in (2, 1, 3, 0):
+                yy = (y + off) % 4
+
+                def sum_a(zz, carry):
+                    t = g32[n, x, zz, yy, :p, :]
+                    for k in range(3):
+                        t = t + ra[k, yy, zz].astype(F32)
+                    ha[yy, zz] = t
+                    ha16[yy, zz] = t.astype(BF16)
+                    return carry
+                lax.fori_loop(0, 4, sum_a, 0)
+                if off:
+                    middle[n][0].push(ha16.at[yy], r2a.at[off - 1], on_y(off))
+
+        def part_c(i):
+            if i < len(heavy[n][2]):
+                heavy[n][2][i].arrive()
+            slow = (planar(n, x, y)[0] + order[i]) % 4
 
             def sum_c(fast, carry):
                 xs, yy = planar(n, slow, fast)
@@ -294,8 +306,16 @@
                 hc16[slow, fast] = t.astype(BF16)
                 return carry
             lax.fori_loop(0, 4, sum_c, 0)
-            if off:
-                middle[n][2].push(hc16.at[slow], r2c.at[off - 1], on_slow[n](off))
+            if i < 3:
+                middle[n][2].push(hc16.at[slow], r2c.at[order[i] - 1], on_slow[n](order[i]))
+
+        for i in range(3):
+            part_b(i)
+        part_a()
+        for i in range(3):
+            part_c(i)
+        part_b(3)
+        part_c(3)
 
     last = [None, None]
 
@@ -363,9 +383,11 @@
                 next_ref[:, cols] = (1.0 - ema_rate) * anchor_ref[:, cols] + ema_rate * (
                     policy_ref[:, cols] - step_size * g)
 
-    started = third_start(0)
+    second = second_start(0)
+    started = third_start(0, second)
+    second = second_start(1)
     rest0 = third_forward(0, started)
-    started = third_start(1)
+    started = third_start(1, second)
     own_x.wait()
     own_cot.wait()
     for group in sib:
@@ -373,8 +395,8 @@
     for group in rest0:
         group.arrive()
     first_product(0)
+    make_signal(0)
     rest1 = third_forward(1, started)
-    make_signal(0)
     for i in range(4):
         second_product(0, i)
     for group in rest1:
@@ -385,12 +407,12 @@
         second_product(1, i)
     first_sums(0)
     second_product(1, 3)
+    first_sums(1)
     second_sums(0)
-    first_sums(1)
+    second_sums(1)
     last_sums(0)
-    second_sums(1)
+    last_sums(1)
     finish(0)
-    last_sums(1)
     finish(1)
 
     for group in groups:
@@ -401,6 +423,9 @@
     vmem = pl.BlockSpec(memory_space=pltpu.VMEM)
     hbm = pl.BlockSpec(memory_space=pl.ANY)
     scratch = [
+        pltpu.VMEM((1, LEN), jnp.int32),
+        pltpu.VMEM((ROWS, KVW), F32),
+        pltpu.VMEM((ROWS, KVW), F32),
         pltpu.VMEM((2 * LEN, D), BF16),
         pltpu.VMEM((SLAB, WIDE), F32),
         pltpu.VMEM((D, WIDE), BF16),
@@ -411,8 +436,8 @@
         pltpu.VMEM((2, 4, 4, 4, PACK, 128), F32),
         pltpu.VMEM((2, 4, 80, 128), F32),
     ]
-    for p, q, r in CUTS:
-        scratch += [pltpu.VMEM((4, 4, 4, m, 128), BF16) for m in (p, q, r)]
+    for ag, (p, q, r) in zip(AG, CUTS):
+        scratch += [pltpu.VMEM((4, 4, 4, m, 128), BF16) for m in ag]
         scratch += [pltpu.VMEM((4, 4, 4, m, 128), BF16) for m in (p, q, r)]
         scratch += [pltpu.VMEM((3, 4, 4, m, 128), BF16) for m in (p, q)]
         scratch += [pltpu.VMEM((7, 4, 4, 16, 128), BF16)]
@@ -423,12 +448,12 @@
                      (pltpu.VMEM((4, 16, 128), F32), pltpu.VMEM((4, 16, 128), BF16)))]
         scratch += [(pltpu.VMEM((7, 64, 128), BF16), pltpu.VMEM((3, 16, 128), BF16))]
     scratch += [pltpu.SemaphoreType.DMA((NSEM,)), pltpu.SemaphoreType.DMA((NSEM,)),
-                pltpu.SemaphoreType.DMA((2,))]
+                pltpu.SemaphoreType.DMA((5,))]
     rows = jax.ShapeDtypeStruct((ROWS, KVW), F32)
     return pl.pallas_call(
         kernel,
         out_shape=(rows, rows),
-        in_specs=[hbm, hbm, vmem, vmem, vmem],
+        in_specs=[hbm] * 5,
         out_specs=(vmem, vmem),
         scratch_shapes=scratch,
         compiler_params=pltpu.CompilerParams(

time: 90.4 us -> 84.9 us (0.939)
  Pallas kernels: 86.2 us -> 80.7 us
    pallas_call x1, Pallas kernels: 86.2 us -> 80.7 us  [shards(): pl.pallas_call(kernel, out_shape=(rows, rows), in_specs=[hbm] * 5, out_sp...]
where the time goes in v4:
time: 84.9 us; the launch traced here: 84.7 us
  Pallas kernels  80.7 us (95%)
  local copies, waits for them, and re-layouts  3.39 us (4%)
    pallas_call x1, Pallas kernels, shards(): pl.pallas_call(kernel, out_shape=(rows, rows), in_specs=[hbm] * 5, out_sp...  80.7 us
    unnamed x2, local copies, waits for them, and re-layouts  3.39 us

profile of v4, /device:TPU:1, one launch (start us, length us, event | category | flops | bytes accessed | tf_op | source)
XLA Modules:
  0.0 84.7 jit_solution(16903624021665249007)
XLA Ops:
  0.6 80.7 %policy_step.1 = (f32[72,1024]{1,0:T(8,128)}, f32[72,1024]{1,0:T(8,128)}) custom-call(bf16[1,768,4608]{2,1,0:T(8,128)(2,1)} %x_hbm.1, bf16[1,768,1024]{2,1,0:T(8,128)(2,1)} %cot_hbm.1, s32[1,768]{1,0:T(1,128)} %mask_hbm.1, f32[72,1024]{1,0:T(8,128)} %policy_hbm.1, f32[72,1024]{1,0:T(8,128)} %anchor_hbm.1), custom_call_target="tpu_custom_call" | custom-call | flops 14495514624 | bytes 20971520 | tf_op jit(solution)/shard_map/policy_step/pallas_call | solution.py:453
  81.3 1.7 %copy.9 = f32[72,1024]{1,0:T(8,128)} copy(f32[72,1024]{1,0:T(8,128)} %get-tuple-element.4) | data formatting | bytes 589824
  83.0 1.7 %copy.10 = f32[72,1024]{1,0:T(8,128)} copy(f32[72,1024]{1,0:T(8,128)} %get-tuple-element.5) | data formatting | bytes 589824

commit v5 on v4

--- a/solution.py
+++ b/solution.py
@@ -419,6 +419,20 @@
         group.sent()
 
 
+def hand_over(a_in, b_in, a_out, b_out, held, sems):
+    jobs = []
+    for n, (src, dst) in enumerate(((a_in, a_out), (b_in, b_out))):
+        jobs.append((pltpu.make_async_copy(src, held.at[n], sems.at[n]),
+                     pltpu.make_async_copy(held.at[n], dst, sems.at[2 + n])))
+    for fetch, _ in jobs:
+        fetch.start()
+    for fetch, store in jobs:
+        fetch.wait()
+        store.start()
+    for _, store in jobs:
+        store.wait()
+
+
 def shards(inputs, cotangent, response_mask, policy, anchor):
     vmem = pl.BlockSpec(memory_space=pltpu.VMEM)
     hbm = pl.BlockSpec(memory_space=pl.ANY)
@@ -450,7 +464,7 @@
     scratch += [pltpu.SemaphoreType.DMA((NSEM,)), pltpu.SemaphoreType.DMA((NSEM,)),
                 pltpu.SemaphoreType.DMA((5,))]
     rows = jax.ShapeDtypeStruct((ROWS, KVW), F32)
-    return pl.pallas_call(
+    sums = pl.pallas_call(
         kernel,
         out_shape=(rows, rows),
         in_specs=[hbm] * 5,
@@ -461,6 +475,15 @@
         cost_estimate=pl.CostEstimate(flops=4 * LEN * D * KVW, bytes_accessed=20 * 2**20, transcendentals=0),
         name="policy_step",
     )(inputs, cotangent, response_mask, policy, anchor)
+    return pl.pallas_call(
+        hand_over,
+        out_shape=(rows, rows),
+        in_specs=[hbm, hbm],
+        out_specs=(hbm, hbm),
+        scratch_shapes=[pltpu.VMEM((2, ROWS, KVW), F32), pltpu.SemaphoreType.DMA((4,))],
+        compiler_params=pltpu.CompilerParams(vmem_limit_bytes=62 * 2**20),
+        name="hand_over",
+    )(*sums)
 
 
 def solution(mesh):

time: 84.9 us -> 83.3 us (0.981)
  local copies, waits for them, and re-layouts: 3.39 us -> 0 us
  Pallas kernels: 80.7 us -> 82.5 us
    unnamed x2 -> x0, local copies, waits for them, and re-layouts: 3.39 us -> none
    pallas_call x0 -> x1, Pallas kernels: none -> 1.81 us  [shards(): pl.pallas_call(hand_over, out_shape=(rows, rows), in_specs=[hbm, hbm], ou...]
where the time goes in v5:
time: 83.3 us; the launch traced here: 83.2 us
  Pallas kernels  82.5 us (99%)
    pallas_call x1, Pallas kernels, shards(): pl.pallas_call(kernel, out_shape=(rows, rows), in_specs=[hbm] * 5, out_sp...  80.7 us
    pallas_call x1, Pallas kernels, shards(): pl.pallas_call(hand_over, out_shape=(rows, rows), in_specs=[hbm, hbm], ou...  1.81 us

profile of v5, /device:TPU:1, one launch (start us, length us, event | category | flops | bytes accessed | tf_op | source)
XLA Modules:
  0.0 83.2 jit_solution(699683172493518723)
XLA Ops:
  0.6 80.7 %policy_step.1 = (f32[72,1024]{1,0:T(8,128)}, f32[72,1024]{1,0:T(8,128)}) custom-call(bf16[1,768,4608]{2,1,0:T(8,128)(2,1)} %x_hbm.1, bf16[1,768,1024]{2,1,0:T(8,128)(2,1)} %cot_hbm.1, s32[1,768]{1,0:T(1,128)} %mask_hbm.1, f32[72,1024]{1,0:T(8,128)} %policy_hbm.1, f32[72,1024]{1,0:T(8,128)} %anchor_hbm.1), custom_call_target="tpu_custom_call" | custom-call | flops 14495514624 | bytes 20971520 | tf_op jit(solution)/shard_map/policy_step/pallas_call | solution.py:467
  81.3 1.8 %hand_over.1 = (f32[72,1024]{1,0:T(8,128)}, f32[72,1024]{1,0:T(8,128)}) custom-call(f32[72,1024]{1,0:T(8,128)} %get-tuple-element.4.a_in, f32[72,1024]{1,0:T(8,128)} %get-tuple-element.5.b_in), custom_call_target="tpu_custom_call" | custom-call | tf_op jit(solution)/shard_map/hand_over/pallas_call | solution.py:478

commit v6 on v4

--- a/solution.py
+++ b/solution.py
@@ -26,7 +26,7 @@
 NSEM = 64
 
 
-def kernel(x_hbm, cot_hbm, mask_hbm, policy_hbm, anchor_hbm, grad_ref, next_ref,
+def kernel(x_hbm, cot_hbm, mask_hbm, policy_hbm, anchor_hbm, grad_ref,
            mask_ref, policy_ref, anchor_ref, xv, stage, dcol, spread, cot, sig_t, scale, g32, fin, *rest):
     lanes = [rest[17 * i:17 * (i + 1)] for i in range(2)]
     ssem, rsem, loc = rest[34:]
@@ -378,10 +378,7 @@
             for half in range(2):
                 begin = core * HALF + n * WIDE + half * 128
                 cols = slice(begin, begin + 128)
-                g = v[ROWS * half:ROWS * (half + 1)]
-                grad_ref[:, cols] = g
-                next_ref[:, cols] = (1.0 - ema_rate) * anchor_ref[:, cols] + ema_rate * (
-                    policy_ref[:, cols] - step_size * g)
+                grad_ref[:, cols] = v[ROWS * half:ROWS * (half + 1)]
 
     second = second_start(0)
     started = third_start(0, second)
@@ -395,8 +392,8 @@
     for group in rest0:
         group.arrive()
     first_product(0)
+    rest1 = third_forward(1, started)
     make_signal(0)
-    rest1 = third_forward(1, started)
     for i in range(4):
         second_product(0, i)
     for group in rest1:
@@ -417,6 +414,23 @@
 
     for group in groups:
         group.sent()
+
+
+def hand_over(sum_in, policy_in, anchor_in, grad_out, next_out, held, sems):
+    fetches = [pltpu.make_async_copy(src, held.at[n], sems.at[n])
+               for n, src in enumerate((sum_in, policy_in, anchor_in))]
+    for fetch in fetches:
+        fetch.start()
+    fetches[0].wait()
+    stores = [pltpu.make_async_copy(held.at[0], grad_out, sems.at[3]),
+              pltpu.make_async_copy(held.at[3], next_out, sems.at[4])]
+    stores[0].start()
+    fetches[1].wait()
+    fetches[2].wait()
+    held[3] = (1.0 - ema_rate) * held[2] + ema_rate * (held[1] - step_size * held[0])
+    stores[1].start()
+    for store in stores:
+        store.wait()
 
 
 def shards(inputs, cotangent, response_mask, policy, anchor):
@@ -450,17 +464,26 @@
     scratch += [pltpu.SemaphoreType.DMA((NSEM,)), pltpu.SemaphoreType.DMA((NSEM,)),
                 pltpu.SemaphoreType.DMA((5,))]
     rows = jax.ShapeDtypeStruct((ROWS, KVW), F32)
-    return pl.pallas_call(
+    total = pl.pallas_call(
         kernel,
-        out_shape=(rows, rows),
+        out_shape=rows,
         in_specs=[hbm] * 5,
-        out_specs=(vmem, vmem),
+        out_specs=vmem,
         scratch_shapes=scratch,
         compiler_params=pltpu.CompilerParams(
             collective_id=0, has_side_effects=True, vmem_limit_bytes=62 * 2**20),
         cost_estimate=pl.CostEstimate(flops=4 * LEN * D * KVW, bytes_accessed=20 * 2**20, transcendentals=0),
         name="policy_step",
     )(inputs, cotangent, response_mask, policy, anchor)
+    return pl.pallas_call(
+        hand_over,
+        out_shape=(rows, rows),
+        in_specs=[hbm] * 3,
+        out_specs=(hbm, hbm),
+        scratch_shapes=[pltpu.VMEM((4, ROWS, KVW), F32), pltpu.SemaphoreType.DMA((5,))],
+        compiler_params=pltpu.CompilerParams(vmem_limit_bytes=62 * 2**20),
+        name="hand_over",
+    )(total, policy, anchor)
 
 
 def solution(mesh):

time: 84.9 us -> 82.6 us (0.973)
  local copies, waits for them, and re-layouts: 3.39 us -> 0 us
  Pallas kernels: 80.7 us -> 81.8 us
    unnamed x2 -> x0, local copies, waits for them, and re-layouts: 3.39 us -> none
    pallas_call x1 -> x2, Pallas kernels: 80.7 us -> 81.8 us  [the longest x1 79.9 us: shards(): pl.pallas_call(kernel, out_shape=rows, in_specs=[hbm] * 5, out_specs=vmem...]
where the time goes in v6:
time: 82.6 us; the launch traced here: 82.5 us
  Pallas kernels  81.8 us (99%)
    pallas_call x1, Pallas kernels, shards(): pl.pallas_call(kernel, out_shape=rows, in_specs=[hbm] * 5, out_specs=vmem...  79.9 us
    pallas_call x1, Pallas kernels, shards(): pl.pallas_call(hand_over, out_shape=(rows, rows), in_specs=[hbm] * 3, out...  1.97 us

profile of v6, /device:TPU:1, one launch (start us, length us, event | category | flops | bytes accessed | tf_op | source)
XLA Modules:
  0.0 82.5 jit_solution(3175659569011646406)
XLA Ops:
  0.6 79.9 %policy_step.1.sum_in = f32[72,1024]{1,0:T(8,128)} custom-call(bf16[1,768,4608]{2,1,0:T(8,128)(2,1)} %x_hbm.1, bf16[1,768,1024]{2,1,0:T(8,128)(2,1)} %cot_hbm.1, s32[1,768]{1,0:T(1,128)} %mask_hbm.1, f32[72,1024]{1,0:T(8,128)} %policy_in.1, f32[72,1024]{1,0:T(8,128)} %anchor_in.1), custom_call_target="tpu_custom_call" | custom-call | flops 14495514624 | bytes 20971520 | tf_op jit(solution)/shard_map/policy_step/pallas_call | solution.py:467
  80.5 2.0 %hand_over.1 = (f32[72,1024]{1,0:T(8,128)}, f32[72,1024]{1,0:T(8,128)}) custom-call(f32[72,1024]{1,0:T(8,128)} %policy_step.1.sum_in, f32[72,1024]{1,0:T(8,128)} %policy_in.1, f32[72,1024]{1,0:T(8,128)} %anchor_in.1), custom_call_target="tpu_custom_call" | custom-call | tf_op jit(solution)/shard_map/hand_over/pallas_call | solution.py:478
